TPU v7x, 256 devices: a whole 4x4x8 slice. The times are simulated.
256 devices in a mesh: ka: 8 (over z), band: 8 (over x_lo, y), fit: 4 (over x_hi, core).
Axes of the slice: x: 4 (x_hi: 2, x_lo: 2; x = x_hi * 2 + x_lo), y: 4, z: 8, core: 2. Of those that a mesh axis runs over, the one named last changes fastest.
Arguments:
- fitted: bfloat16 [8, 2, 2048, 24576], P('ka', None, 'fit', 'band'), may hold values from -6 to 6
- omega: float32 [6, 2048], P(None, 'fit'), may hold values from 0.05 to 1
- coefficients: float32 [2, 6], replicated, may hold values from 0.2 to 1
- partner: int32 [8], replicated, may hold values from 0 to 7, as said below
Outputs:
- pair_v: float32 [2, 8, 48, 48], P(None, 'ka', 'band')
- pair_x: float32 [2, 8, 48, 48], P(None, 'ka', 'band')
Inputs may be any that keep to these rules, and one draw needn't show every extreme that they name: partner is a permutation that maps the 1 k-points of each aligned block b (k-points b * 1 to b + 1 - 1) onto those of block (b + t) mod (8), in some order, for one whole t with 1 <= t < 8 shared by all blocks.
All inputs are finite; a program needn't handle non-finite values.
Results may differ from a plain program's by a relative error of at most 0.0029.
Values may be sent and summed in bfloat16 or wider, within the bound.
No kernel may reach another device: no remote copies, remote signals or barrier semaphores. Data moves between devices by JAX's collectives and lax.ppermute only.
A program may use at most 192 MiB of HBM per device.

v0:
```python
import functools
import math

import jax
import jax.numpy as jnp
import numpy as np
from jax import lax
from jax.experimental import pallas as pl
from jax.experimental.pallas import tpu as pltpu
from jax.sharding import PartitionSpec as P

NOCC = 48
NCABS = 512
NAUX = 2048
GROUP = 8
WIDTH = GROUP * NOCC


def shifted(value, axis, by):
    devices = lax.axis_size(axis)
    return lax.ppermute(value, axis, [(i, (i + by) % devices) for i in range(devices)])


def fold_matrix(owners):
    rows = NOCC // owners
    column, row = np.arange(4 * WIDTH), np.arange(4 * NOCC)
    term, within = row % (4 * rows) // rows, row // (4 * rows) * rows + row % rows
    column_key = jnp.asarray(column // WIDTH * NOCC + column % NOCC, jnp.int32)
    row_key = jnp.asarray(term * NOCC + within, jnp.int32)
    return (column_key[:, None] == row_key[None, :]).astype(jnp.bfloat16)


def add_product(a_ref, b_ref, w_ref, scaled, total, begins):
    depth = w_ref.shape[0]
    rows = scaled.shape[0] // 2

    @pl.loop(0, depth // rows)
    def _(at):
        upper = pl.ds(pl.multiple_of(at * rows, rows), rows)
        lower = pl.ds(pl.multiple_of(depth + at * rows, rows), rows)
        real = a_ref[upper].astype(jnp.float32)
        imag = a_ref[lower].astype(jnp.float32)
        for operator in range(2):
            w = w_ref[upper, operator : operator + 1]
            a0 = (real * w).astype(jnp.bfloat16)
            a1 = (imag * w).astype(jnp.bfloat16)
            left = slice(2 * operator * WIDTH, (2 * operator + 1) * WIDTH)
            right = slice((2 * operator + 1) * WIDTH, (2 * operator + 2) * WIDTH)
            scaled[:rows, left] = a0
            scaled[rows:, left] = a1
            scaled[:rows, right] = a1
            scaled[rows:, right] = -a0
        before = jnp.where(begins & (at == 0), 0.0, total[...])
        total[...] = before + lax.dot_general(
            jnp.concatenate([b_ref[upper], b_ref[lower]]),
            scaled[...],
            (((0,), (0,)), ((), ())),
            preferred_element_type=jnp.float32,
        )


def folded_total(total, fold_ref):
    column_band = lax.broadcasted_iota(jnp.int32, (1, WIDTH), 1) // NOCC

    def add_term(term, result):
        columns = pl.ds(pl.multiple_of(term * WIDTH, WIDTH), WIDTH)
        diagonal = jnp.zeros((NOCC, WIDTH), jnp.float32)
        for band in range(GROUP):
            block = total[band * NOCC : (band + 1) * NOCC, columns]
            diagonal = jnp.where(column_band == band, block, diagonal)
        high = diagonal.astype(jnp.bfloat16)
        rest = diagonal - high.astype(jnp.float32)
        middle = rest.astype(jnp.bfloat16)
        low = (rest - middle.astype(jnp.float32)).astype(jnp.bfloat16)
        folded = jnp.dot(
            jnp.concatenate([high, middle, low]),
            fold_ref[columns, :],
            preferred_element_type=jnp.float32,
        )
        high, middle, low = (folded[n * NOCC : (n + 1) * NOCC] for n in range(3))
        return result + (high + (middle + low))

    zero = jnp.zeros((NOCC, 4 * NOCC), jnp.float32)
    return lax.fori_loop(0, 4, add_term, zero, unroll=True).T


A, B, SLOT, BEGINS, ENDS, A_COLUMN, B_COLUMN = range(7)


def list_kernel(places, pairs, *refs):
    arrays = len(refs) - 8
    w_ref, fold_ref, so_far_ref, out_ref, buffer, scaled, total, sems = refs[arrays:]
    step = pl.program_id(0)

    begin = jnp.where(step == 0, 0, 2 * step + 2)
    end = 2 * jnp.minimum(step + 2, pl.num_programs(0))

    @pl.loop(begin, end)
    def _(at):
        which, operand = at // 2, at % 2
        wanted = pairs[A + operand, which]
        column = pl.multiple_of(pairs[A_COLUMN + operand, which] * WIDTH, WIDTH)
        for place, parts in enumerate(places):

            @pl.when(wanted == place)
            def _():
                rows = buffer.shape[2] // len(parts)
                for at, (array, row) in enumerate(parts):
                    pltpu.make_async_copy(
                        refs[array].at[pl.ds(row, rows), pl.ds(column, WIDTH)],
                        buffer.at[which % 2, operand, pl.ds(at * rows, rows)],
                        sems.at[which % 2, operand],
                    ).start()

    slot = step % 2
    for operand in range(2):
        here = buffer.at[slot, operand]
        pltpu.make_async_copy(here, here, sems.at[slot, operand]).wait()
    begins = pairs[BEGINS, step] != 0
    add_product(buffer.at[slot, 0], buffer.at[slot, 1], w_ref, scaled, total, begins)

    @pl.when(pairs[ENDS, step] != 0)
    def _():
        terms = folded_total(total, fold_ref).reshape(out_ref.shape)
        out_ref[...] = so_far_ref[...] + terms


def list_terms(pairs, views, weights, fold, so_far):
    arrays = []
    places = []
    for parts in views:
        place = []
        for array, row in parts:
            known = [at for at, other in enumerate(arrays) if other is array]
            place.append((known[0] if known else len(arrays), row))
            if not known:
                arrays.append(array)
        places.append(place)
    _, owners, rows, _ = so_far.shape
    depth = weights.shape[0]
    block = pl.BlockSpec((1, owners, rows, NOCC), lambda g, s: (s[SLOT, g], 0, 0, 0))
    return pl.pallas_call(
        functools.partial(list_kernel, places),
        grid_spec=pltpu.PrefetchScalarGridSpec(
            num_scalar_prefetch=1,
            grid=(pairs.shape[1],),
            in_specs=[pl.BlockSpec(memory_space=pl.ANY)] * len(arrays)
            + [
                pl.BlockSpec((depth, 2), lambda g, s: (0, 0)),
                pl.BlockSpec((4 * WIDTH, 4 * NOCC), lambda g, s: (0, 0)),
                block,
            ],
            out_specs=block,
            scratch_shapes=[
                pltpu.VMEM((2, 2, 2 * depth, WIDTH), jnp.bfloat16),
                pltpu.VMEM((depth, 4 * WIDTH), jnp.bfloat16),
                pltpu.VMEM((WIDTH, 4 * WIDTH), jnp.float32),
                pltpu.SemaphoreType.DMA((2, 2)),
            ],
        ),
        out_shape=jax.ShapeDtypeStruct(so_far.shape, jnp.float32),
        input_output_aliases={len(arrays) + 3: 0},
        compiler_params=pltpu.CompilerParams(vmem_limit_bytes=32 * 2**20),
        cost_estimate=pl.CostEstimate(flops=0, bytes_accessed=0, transcendentals=0),
        name="list_terms",
    )(pairs, *arrays, weights, fold, so_far)


def cut_kernel(groups, me_ref, x_ref, *refs):
    *out_refs, sems = refs
    columns = x_ref.shape[1] // WIDTH
    copies = []
    for pieces, out_ref in zip(groups, out_refs):
        row = 0
        for shift, begin, rows in pieces:
            column = pl.multiple_of(lax.rem(me_ref[0] + shift, columns) * WIDTH, WIDTH)
            source = x_ref.at[pl.ds(begin, rows), pl.ds(column, out_ref.shape[1])]
            target = out_ref.at[pl.ds(row, rows)]
            copies.append(pltpu.make_async_copy(source, target, sems.at[len(copies)]))
            row += rows
    for copy in copies:
        copy.start()
    for copy in copies:
        copy.wait()


def cut(x, me, *groups, blocks=1):
    shapes = [(sum(rows for _, _, rows in pieces), blocks * WIDTH) for pieces in groups]
    count = sum(len(pieces) for pieces in groups)
    return pl.pallas_call(
        functools.partial(cut_kernel, groups),
        grid_spec=pltpu.PrefetchScalarGridSpec(
            num_scalar_prefetch=1,
            grid=(1,),
            in_specs=[pl.BlockSpec(memory_space=pl.ANY)],
            out_specs=[pl.BlockSpec(shape, lambda g, me: (0, 0)) for shape in shapes],
            scratch_shapes=[pltpu.SemaphoreType.DMA((count,))],
        ),
        out_shape=[jax.ShapeDtypeStruct(shape, x.dtype) for shape in shapes],
        compiler_params=pltpu.CompilerParams(vmem_limit_bytes=32 * 2**20),
        cost_estimate=pl.CostEstimate(flops=0, bytes_accessed=0, transcendentals=0),
        name="cut",
    )(me.reshape(1), x)


def weights_of(coefficients, omega):
    kernel = jnp.dot(
        coefficients, omega, precision=lax.Precision.HIGHEST, preferred_element_type=jnp.float32
    ) / math.sqrt(NAUX * NCABS)
    return kernel.T


def reduced(terms):
    owners, copies = lax.axis_size("band"), lax.axis_size("fit")
    rows = terms.shape[1]
    sent = jnp.broadcast_to(terms[:, None], (owners, copies, rows, NOCC))
    sent = sent.reshape(owners * copies, rows, NOCC)
    return lax.all_to_all(sent, ("band", "fit"), 0, 0, tiled=True).sum(0)


def neighbours(distance, x, coefficients, omega):
    owners = lax.axis_size("band")
    rows = 4 * NOCC // owners
    fold = fold_matrix(owners)
    weights = weights_of(coefficients, omega)
    height = x.shape[0]
    half = x.shape[1] // WIDTH // 2
    upward = distance == 1
    start = jnp.zeros((), jnp.int32)
    pieces = []
    at = 0
    for size in (half - half // 4, half // 4):
        low, high = [(at, 0, height)], [(half + at, 0, height)]
        up, down = cut(x, start, low, high, blocks=size)
        views = [[(shifted(up, "ka", 1), 0)], [(shifted(down, "ka", -1), 0)], [(x, 0)]]
        pieces.append((at, size, views))
        at += size

    def table(at, size, foreign):
        def columns(came, first):
            result = np.zeros((7, size), np.int32)
            place, column = (A, A_COLUMN) if foreign else (B, B_COLUMN)
            result[place], result[column] = came, np.arange(size)
            place, column = (B, B_COLUMN) if foreign else (A, A_COLUMN)
            result[place], result[column] = 2, first + np.arange(size)
            result[SLOT], result[BEGINS, 0], result[ENDS, -1] = int(foreign), 1, 1
            return result

        up, down = columns(0, at), columns(1, half + at)
        return jnp.where(upward, *((up, down) if foreign else (down, up)))

    terms = jnp.zeros((2, owners, rows, NOCC), jnp.float32)
    for at, size, views in pieces:
        pairs = jnp.concatenate([table(at, size, True), table(at, size, False)], axis=1)
        terms = list_terms(pairs, views, weights, fold, terms)
    own, foreign = terms[0], terms[1]
    own += shifted(jnp.where(upward, foreign, 0.0), "ka", -1)
    own += shifted(jnp.where(upward, 0.0, foreign), "ka", 1)
    return reduced(own)


def listed_pairs(cycle, distance):
    far = cycle // 2

    def waits(d):
        blocks = (d, (d + distance) % cycle)
        return 2 if far in blocks else int(2 in blocks or cycle - 2 in blocks)

    return sorted(range(cycle), key=lambda d: (waits(d), d))


def spread(distance, x, coefficients, omega):
    owners = lax.axis_size("band")
    rows = 4 * NOCC // owners
    fold = fold_matrix(owners)
    weights = weights_of(coefficients, omega)
    cycle = lax.axis_size("ka")
    me = lax.axis_index("ka")
    size = x.shape[0]
    part = size // 2

    def whole(d):
        return (d % cycle, 0, size)

    up_long, down_long = cut(
        x, me, [whole(3), (4, 0, part)], [whole(-3), (4, part, part)]
    )
    up_short, down_short = cut(x, me, [whole(2), whole(1)], [whole(-2), whole(-1)])
    own = cut(x, me, [whole(0)])[0]

    def ring(long, short, step):
        first = shifted(long, "ka", step)
        first, _ = lax.optimization_barrier((first, short))
        short = shifted(short, "ka", step)
        second = shifted(first, "ka", step)
        third = shifted(second, "ka", step)
        return short, shifted(short[:size], "ka", step), third, shifted(third[size:], "ka", step)

    up_short, up_two, up_long, up_far = ring(up_long, up_short, 1)
    down_short, down_two, down_long, down_far = ring(down_long, down_short, -1)

    firsts = np.array([listed_pairs(cycle, max(t, 1)) for t in range(cycle)], np.int32)
    firsts = jnp.asarray(firsts)[distance]

    def table(first):
        one, none = jnp.ones_like(first), jnp.zeros_like(first)
        second, owner = (first + distance) % cycle, (first + me) % cycle
        return jnp.stack([first, second, owner, one, one, none, none])

    views = [[(own, 0)]] * cycle
    views[1], views[7] = [(down_short, size)], [(up_short, size)]
    views[3], views[5] = [(down_long, 0)], [(up_long, 0)]
    terms = jnp.zeros((cycle, owners, rows, NOCC), jnp.float32)
    terms = list_terms(table(firsts[:2]), views, weights, fold, terms)
    up_two, down_two, terms = lax.optimization_barrier((up_two, down_two, terms))
    views[2], views[6] = [(down_two, 0)], [(up_two, 0)]
    terms = list_terms(table(firsts[2:6]), views, weights, fold, terms)
    up_far, down_far, terms = lax.optimization_barrier((up_far, down_far, terms))
    views[4] = [(up_far, 0), (down_far, 0)]
    terms = list_terms(table(firsts[6:]), views, weights, fold, terms)
    sent = terms.reshape(cycle * owners, rows, NOCC)
    mine = lax.all_to_all(sent, ("ka", "band"), 0, 0, tiled=True).sum(0)
    return lax.all_gather(mine, "fit").sum(0)


def shards(fitted, omega, coefficients, partner):
    cycle = lax.axis_size("ka")
    distance = partner[0]
    away = (distance != 1) & (distance != cycle - 1)
    x = fitted.reshape(2 * fitted.shape[2], fitted.shape[3])
    total = lax.cond(away, spread, neighbours, distance, x, coefficients, omega)
    total = total.reshape(2, 2, 1, -1, NOCC)
    return (total[0], total[1])


def solution(mesh):
    placed = (P("ka", None, "fit", "band"), P(None, "fit"), P(), P())
    return jax.shard_map(
        shards,
        mesh=mesh,
        in_specs=placed,
        out_specs=(P(None, "ka", "band", None), P(None, "ka", "band", None)),
        check_vma=False,
    )
```

profile of v0, /device:TPU:1, one launch (start us, length us, event | category | flops | bytes accessed | tf_op | source)
XLA Modules:
  0.0 195.6 jit_solution(2178629115269803859)
XLA Ops:
  1.9 192.5 %conditional.1 = (f32[24,48]{1,0:T(8,128)S(1)}) conditional(s32[]{:T(128)} %convert_element_type.9, (s32[]{:T(128)}, (), (), (), (), /*index=5*/bf16[1024,3072]{1,0:T(8,128)(2,1)}, f32[6,512]{1,0:T(8,128)}, f32[2,6]{1,0:T(2,128)}, s32[1536]{0:T(1024)}, s32[192]{0:T(256)}, /*index=10*/(), (), (), ()) %tuple.73, (s32[]{:T(128)}, (), ...), branch_computations={%region_0.2_spmd, %region_2.5_spmd} | conditional | flops 740806 | bytes 90199080 | solution.py:331
  2.0 1.8 cut.9
  3.8 2.5 %collective-permute-start.13 = (bf16[1536,384]{1,0:T(8,128)(2,1)S(1)}, bf16[1536,384]{1,0:T(8,128)(2,1)S(1)}, u32[]{:S(2)}, u32[]{:S(2)}) collective-permute-start(bf16[1536,384]{1,0:T(8,128)(2,1)S(1)} %get-tuple-element.70), channel_id=1, source_target_pairs={{0,32},{32,64},{64,96},{96,128},{128,160},{160,192},{192,224},{224... | collective-permute-start | bytes 3538952 | tf_op jit(solution)/shard_map/cond/branch_1_fun/ppermute | solution.py:21
  6.3 4.0 %collective-permute-start.10 = (bf16[1536,384]{1,0:T(8,128)(2,1)S(1)}, bf16[1536,384]{1,0:T(8,128)(2,1)S(1)}, u32[]{:S(2)}, u32[]{:S(2)}) collective-permute-start(bf16[1536,384]{1,0:T(8,128)(2,1)S(1)} %get-tuple-element.68), channel_id=1, source_target_pairs={{0,224},{32,0},{64,32},{96,64},{128,96},{160,128},{192,160},{224,1... | collective-permute-start | bytes 3538952 | tf_op jit(solution)/shard_map/cond/branch_1_fun/ppermute | solution.py:21
  10.4 2.1 %cut.8 = (bf16[2048,384]{1,0:T(8,128)(2,1)}, bf16[2048,384]{1,0:T(8,128)(2,1)}) custom-call(s32[1]{0:T(128)} %bitcast.4.me_ref, bf16[1024,3072]{1,0:T(8,128)(2,1)S(1)} %copy-done.3), custom_call_target="tpu_custom_call" | custom-call | tf_op jit(solution)/shard_map/cond/branch_1_fun/cut/pallas_call | solution.py:190
  12.5 23.5 %collective-permute-done.13 = bf16[1536,384]{1,0:T(8,128)(2,1)S(1)} collective-permute-done((bf16[1536,384]{1,0:T(8,128)(2,1)S(1)}, bf16[1536,384]{1,0:T(8,128)(2,1)S(1)}, u32[]{:S(2)}, u32[]{:S(2)}) %collective-permute-start.13) | collective-permute-done | bytes 1179680 | tf_op jit(solution)/shard_map/cond/branch_1_fun/ppermute | solution.py:21
  36.0 2.7 %collective-permute-start.11 = (bf16[1536,384]{1,0:T(8,128)(2,1)S(1)}, bf16[1536,384]{1,0:T(8,128)(2,1)}, u32[]{:S(2)}, u32[]{:S(2)}) collective-permute-start(bf16[1536,384]{1,0:T(8,128)(2,1)S(1)} %collective-permute-done.10), channel_id=1, source_target_pairs={{0,224},{32,0},{64,32},{96,64},{128,96},{160,128},{192,160},{224,1... | collective-permute-start | bytes 3538952 | tf_op jit(solution)/shard_map/cond/branch_1_fun/ppermute | solution.py:21
  38.6 2.7 %collective-permute-start.6 = (bf16[2048,384]{1,0:T(8,128)(2,1)}, bf16[2048,384]{1,0:T(8,128)(2,1)}, u32[]{:S(2)}, u32[]{:S(2)}) collective-permute-start(bf16[2048,384]{1,0:T(8,128)(2,1)} %get-tuple-element.66), channel_id=1, source_target_pairs={{0,224},{32,0},{64,32},{96,64},{128,96},{160,128},{192,160},{224,1... | collective-permute-start | bytes 4718600 | tf_op jit(solution)/shard_map/cond/branch_1_fun/ppermute | solution.py:21
  41.3 22.2 %collective-permute-done.14 = bf16[1536,384]{1,0:T(8,128)(2,1)} collective-permute-done((bf16[1536,384]{1,0:T(8,128)(2,1)S(1)}, bf16[1536,384]{1,0:T(8,128)(2,1)}, u32[]{:S(2)}, u32[]{:S(2)}) %collective-permute-start.14) | collective-permute-done | bytes 1179680 | tf_op jit(solution)/shard_map/cond/branch_1_fun/ppermute | solution.py:21
  63.5 2.7 %collective-permute-start.12 = (bf16[1536,384]{1,0:T(8,128)(2,1)}, bf16[1536,384]{1,0:T(8,128)(2,1)}, u32[]{:S(2)}, u32[]{:S(2)}) collective-permute-start(bf16[1536,384]{1,0:T(8,128)(2,1)} %collective-permute-done.11), channel_id=1, source_target_pairs={{0,224},{32,0},{64,32},{96,64},{128,96},{160,128},{192,160},{224,1... | collective-permute-start | bytes 3538952 | tf_op jit(solution)/shard_map/cond/branch_1_fun/ppermute | solution.py:21
  66.3 0.7 constant_dynamic-slice_fusion
  67.1 30.0 %collective-permute-done.7.refs_4_.refs_6_.refs_8_ = bf16[2048,384]{1,0:T(8,128)(2,1)S(1)} collective-permute-done((bf16[2048,384]{1,0:T(8,128)(2,1)}, bf16[2048,384]{1,0:T(8,128)(2,1)S(1)}, u32[]{:S(2)}, u32[]{:S(2)}) %collective-permute-start.7) | collective-permute-done | bytes 1572896 | tf_op jit(solution)/shard_map/cond/branch_1_fun/ppermute | solution.py:21
  97.1 1.0 slice.46
  98.1 2.1 %slice.47 = bf16[1024,384]{1,0:T(8,128)(2,1)} slice(bf16[2048,384]{1,0:T(8,128)(2,1)} %collective-permute-done.6.refs_1_), slice={[0:1024], [0:384]} | slice | bytes 1572864 | tf_op jit(solution)/shard_map/cond/branch_1_fun/slice | solution.py:297
  100.2 2.7 %collective-permute-start.9 = (bf16[1024,384]{1,0:T(8,128)(2,1)}, bf16[1024,384]{1,0:T(8,128)(2,1)}, u32[]{:S(2)}, u32[]{:S(2)}) collective-permute-start(bf16[1024,384]{1,0:T(8,128)(2,1)} %slice.47), channel_id=1, source_target_pairs={{0,224},{32,0},{64,32},{96,64},{128,96},{160,128},{192,160},{224,1... | collective-permute-start | bytes 2359304 | tf_op jit(solution)/shard_map/cond/branch_1_fun/ppermute | solution.py:21
  103.0 1.2 cut.7.refs_0_
  104.2 0.9 copy-done
  105.2 0.6 convolution_multiply_fusion.1.refs_5_.refs_7_.refs_9_
  105.8 16.6 %collective-permute-done.15.refs_3_.refs_4_.refs_6_ = bf16[1536,384]{1,0:T(8,128)(2,1)S(1)} collective-permute-done((bf16[1536,384]{1,0:T(8,128)(2,1)}, bf16[1536,384]{1,0:T(8,128)(2,1)S(1)}, u32[]{:S(2)}, u32[]{:S(2)}) %collective-permute-start.15) | collective-permute-done | bytes 1179680 | tf_op jit(solution)/shard_map/cond/branch_1_fun/ppermute | solution.py:21
  122.5 1.0 slice.49
  123.6 3.0 %collective-permute-start.17 = (bf16[512,384]{1,0:T(8,128)(2,1)S(1)}, bf16[512,384]{1,0:T(8,128)(2,1)S(1)}, u32[]{:S(2)}, u32[]{:S(2)}) collective-permute-start(bf16[512,384]{1,0:T(8,128)(2,1)S(1)} %slice.49), channel_id=1, source_target_pairs={{0,224},{32,0},{64,32},{96,64},{128,96},{160,128},{192,160},{224,1... | collective-permute-start | bytes 1179656 | tf_op jit(solution)/shard_map/cond/branch_1_fun/ppermute | solution.py:21
  126.9 5.8 %list_terms.7.refs_9_ = f32[8,8,24,48]{3,2,1,0:T(8,128)S(1)} custom-call(s32[7,2]{1,0:T(8,128)S(1)} %stack.1.pairs, bf16[1024,384]{1,0:T(8,128)(2,1)S(1)} %copy-done.1, bf16[2048,384]{1,0:T(8,128)(2,1)} %collective-permute-done.6.refs_1_, bf16[1536,384]{1,0:T(8,128)(2,1)} %collective-permute-done.12.refs_2_.refs_3_, ...), custom_call_target="tpu_custom_call", output_to_operand_aliasing={{}: (8, {})} | custom-call | tf_op jit(solution)/shard_map/cond/branch_1_fun/list_terms/pallas_call | solution.py:142
  132.7 6.7 %collective-permute-done.8.refs_5_.refs_7_ = bf16[1024,384]{1,0:T(8,128)(2,1)} collective-permute-done((bf16[1024,384]{1,0:T(8,128)(2,1)}, bf16[1024,384]{1,0:T(8,128)(2,1)}, u32[]{:S(2)}, u32[]{:S(2)}) %collective-permute-start.8) | collective-permute-done | bytes 786464 | tf_op jit(solution)/shard_map/cond/branch_1_fun/ppermute | solution.py:21
  139.3 11.8 %list_terms.8.refs_11_ = f32[8,8,24,48]{3,2,1,0:T(8,128)S(1)} custom-call(s32[7,4]{1,0:T(8,128)S(1)} %stack.2.pairs, bf16[1024,384]{1,0:T(8,128)(2,1)S(1)} %copy-done.1, bf16[2048,384]{1,0:T(8,128)(2,1)} %collective-permute-done.6.refs_1_, bf16[1024,384]{1,0:T(8,128)(2,1)} %collective-permute-done.9.refs_2_, ...), custom_call_target="tpu_custom_call", output_to_operand_aliasing={{}: (10, {})} | custom-call | tf_op jit(solution)/shard_map/cond/branch_1_fun/list_terms/pallas_call | solution.py:142
  151.1 7.0 %list_terms.9 = f32[8,8,24,48]{3,2,1,0:T(8,128)S(1)} custom-call(s32[7,2]{1,0:T(8,128)S(1)} %stack.0.pairs, bf16[1024,384]{1,0:T(8,128)(2,1)S(1)} %copy-done.1, bf16[2048,384]{1,0:T(8,128)(2,1)} %collective-permute-done.6.refs_1_, bf16[1024,384]{1,0:T(8,128)(2,1)} %collective-permute-done.9.refs_2_, ...), custom_call_target="tpu_custom_call", output_to_operand_aliasing={{}: (12, {})} | custom-call | tf_op jit(solution)/shard_map/cond/branch_1_fun/list_terms/pallas_call | solution.py:142
  158.1 0.7 reshape.44
  158.9 20.0 %all_to_all.9 = f32[64,1,1152]{2,1,0:T(1,128)S(1)} all-to-all(f32[64,1,1152]{2,1,0:T(1,128)S(1)} %reshape.44), channel_id=1, replica_groups=mesh['ka'=8,'band'=8,'fit'=4] {'ka','band'}, dimensions={0} | all-to-all | bytes 589824 | tf_op jit(solution)/shard_map/cond/branch_1_fun/all_to_all | solution.py:322
  178.8 0.5 broadcast.98
  179.3 1.3 reduce.1
  181.1 13.1 %all-gather = f32[96,48]{1,0:T(8,128)S(1)} all-gather(f32[24,48]{1,0:T(8,128)S(1)} %reduce_sum.25), channel_id=2, replica_groups=mesh['ka'=8,'band'=8,'fit'=4] {'fit'}, dimensions={0}, use_global_device_ids=true | all-gather | bytes 23040 | tf_op jit(solution)/shard_map/cond/branch_1_fun/all_gather | solution.py:323
  194.4 0.6 squeeze.15
  195.0 0.6 squeeze.16
  (43 shorter events, 1.3 us)
Async XLA Ops:
  1.9 8.4 %copy-start.3 = (bf16[1024,3072]{1,0:T(8,128)(2,1)S(1)}, bf16[1024,3072]{1,0:T(8,128)(2,1)}, u32[]{:S(2)}) copy-start(bf16[1024,3072]{1,0:T(8,128)(2,1)} %get-tuple-element.65.x_ref) | copy-start | bytes 18874372 | tf_op jit(solution)/shard_map/cond
  3.8 32.2 %collective-permute-start.13 = (bf16[1536,384]{1,0:T(8,128)(2,1)S(1)}, bf16[1536,384]{1,0:T(8,128)(2,1)S(1)}, u32[]{:S(2)}, u32[]{:S(2)}) collective-permute-start(bf16[1536,384]{1,0:T(8,128)(2,1)S(1)} %get-tuple-element.70), channel_id=1, source_target_pairs={{0,32},{32,64},{64,96},{96,128},{128,160},{160,192},{192,224},{224... | collective-permute-start | bytes 3538952 | tf_op jit(solution)/shard_map/cond/branch_1_fun/ppermute | solution.py:21
  6.3 59.9 %copy-start.9 = (s32[]{:T(128)S(1)}, s32[]{:T(128)}, u32[]{:S(2)}) copy-start(s32[]{:T(128)} %get-tuple-element.64) | copy-start | bytes 16 | tf_op jit(solution)/shard_map/cond
  6.3 29.6 %collective-permute-start.10 = (bf16[1536,384]{1,0:T(8,128)(2,1)S(1)}, bf16[1536,384]{1,0:T(8,128)(2,1)S(1)}, u32[]{:S(2)}, u32[]{:S(2)}) collective-permute-start(bf16[1536,384]{1,0:T(8,128)(2,1)S(1)} %get-tuple-element.68), channel_id=1, source_target_pairs={{0,224},{32,0},{64,32},{96,64},{128,96},{160,128},{192,160},{224,1... | collective-permute-start | bytes 3538952 | tf_op jit(solution)/shard_map/cond/branch_1_fun/ppermute | solution.py:21
  35.9 27.5 %collective-permute-start.14 = (bf16[1536,384]{1,0:T(8,128)(2,1)S(1)}, bf16[1536,384]{1,0:T(8,128)(2,1)}, u32[]{:S(2)}, u32[]{:S(2)}) collective-permute-start(bf16[1536,384]{1,0:T(8,128)(2,1)S(1)} %collective-permute-done.13), channel_id=1, source_target_pairs={{0,32},{32,64},{64,96},{96,128},{128,160},{160,192},{192,224},{224... | collective-permute-start | bytes 3538952 | tf_op jit(solution)/shard_map/cond/branch_1_fun/ppermute | solution.py:21
  36.0 27.5 %collective-permute-start.11 = (bf16[1536,384]{1,0:T(8,128)(2,1)S(1)}, bf16[1536,384]{1,0:T(8,128)(2,1)}, u32[]{:S(2)}, u32[]{:S(2)}) collective-permute-start(bf16[1536,384]{1,0:T(8,128)(2,1)S(1)} %collective-permute-done.10), channel_id=1, source_target_pairs={{0,224},{32,0},{64,32},{96,64},{128,96},{160,128},{192,160},{224,1... | collective-permute-start | bytes 3538952 | tf_op jit(solution)/shard_map/cond/branch_1_fun/ppermute | solution.py:21
  38.6 58.5 %collective-permute-start.7 = (bf16[2048,384]{1,0:T(8,128)(2,1)}, bf16[2048,384]{1,0:T(8,128)(2,1)S(1)}, u32[]{:S(2)}, u32[]{:S(2)}) collective-permute-start(bf16[2048,384]{1,0:T(8,128)(2,1)} %get-tuple-element.67), channel_id=1, source_target_pairs={{0,32},{32,64},{64,96},{96,128},{128,160},{160,192},{192,224},{224... | collective-permute-start | bytes 4718600 | tf_op jit(solution)/shard_map/cond/branch_1_fun/ppermute | solution.py:21
  38.6 59.5 %collective-permute-start.6 = (bf16[2048,384]{1,0:T(8,128)(2,1)}, bf16[2048,384]{1,0:T(8,128)(2,1)}, u32[]{:S(2)}, u32[]{:S(2)}) collective-permute-start(bf16[2048,384]{1,0:T(8,128)(2,1)} %get-tuple-element.66), channel_id=1, source_target_pairs={{0,224},{32,0},{64,32},{96,64},{128,96},{160,128},{192,160},{224,1... | collective-permute-start | bytes 4718600 | tf_op jit(solution)/shard_map/cond/branch_1_fun/ppermute | solution.py:21
  63.5 58.9 %collective-permute-start.15 = (bf16[1536,384]{1,0:T(8,128)(2,1)}, bf16[1536,384]{1,0:T(8,128)(2,1)S(1)}, u32[]{:S(2)}, u32[]{:S(2)}) collective-permute-start(bf16[1536,384]{1,0:T(8,128)(2,1)} %collective-permute-done.14), channel_id=1, source_target_pairs={{0,32},{32,64},{64,96},{96,128},{128,160},{160,192},{192,224},{224... | collective-permute-start | bytes 3538952 | tf_op jit(solution)/shard_map/cond/branch_1_fun/ppermute | solution.py:21
  63.5 59.0 %collective-permute-start.12 = (bf16[1536,384]{1,0:T(8,128)(2,1)}, bf16[1536,384]{1,0:T(8,128)(2,1)}, u32[]{:S(2)}, u32[]{:S(2)}) collective-permute-start(bf16[1536,384]{1,0:T(8,128)(2,1)} %collective-permute-done.11), channel_id=1, source_target_pairs={{0,224},{32,0},{64,32},{96,64},{128,96},{160,128},{192,160},{224,1... | collective-permute-start | bytes 3538952 | tf_op jit(solution)/shard_map/cond/branch_1_fun/ppermute | solution.py:21
  98.1 41.2 %collective-permute-start.8 = (bf16[1024,384]{1,0:T(8,128)(2,1)}, bf16[1024,384]{1,0:T(8,128)(2,1)}, u32[]{:S(2)}, u32[]{:S(2)}) collective-permute-start(bf16[1024,384]{1,0:T(8,128)(2,1)} %slice.46), channel_id=1, source_target_pairs={{0,32},{32,64},{64,96},{96,128},{128,160},{160,192},{192,224},{224... | collective-permute-start | bytes 2359304 | tf_op jit(solution)/shard_map/cond/branch_1_fun/ppermute | solution.py:21
  100.2 39.1 %collective-permute-start.9 = (bf16[1024,384]{1,0:T(8,128)(2,1)}, bf16[1024,384]{1,0:T(8,128)(2,1)}, u32[]{:S(2)}, u32[]{:S(2)}) collective-permute-start(bf16[1024,384]{1,0:T(8,128)(2,1)} %slice.47), channel_id=1, source_target_pairs={{0,224},{32,0},{64,32},{96,64},{128,96},{160,128},{192,160},{224,1... | collective-permute-start | bytes 2359304 | tf_op jit(solution)/shard_map/cond/branch_1_fun/ppermute | solution.py:21
  103.0 2.2 %copy-start.5 = (f32[6,512]{1,0:T(8,128)S(1)}, f32[6,512]{1,0:T(8,128)}, u32[]{:S(2)}) copy-start(f32[6,512]{1,0:T(8,128)} %get-tuple-element.72) | copy-start | bytes 36868 | tf_op jit(solution)/shard_map/cond
  103.0 2.2 %copy-start.11 = (f32[2,6]{1,0:T(2,128)S(1)}, f32[2,6]{1,0:T(2,128)}, u32[]{:S(2)}) copy-start(f32[2,6]{1,0:T(2,128)} %get-tuple-element.73) | copy-start | bytes 148 | tf_op jit(solution)/shard_map/cond
  104.2 0.9 copy-start
  105.1 21.5 %copy-start.7 = (s32[1536]{0:T(1024)S(1)}, s32[1536]{0:T(1024)}, u32[]{:S(2)}) copy-start(s32[1536]{0:T(1024)} %get-tuple-element.74) | copy-start | bytes 18436 | tf_op jit(solution)/shard_map/cond
  105.1 21.5 %copy-start.13 = (s32[192]{0:T(256)S(1)}, s32[192]{0:T(256)}, u32[]{:S(2)}) copy-start(s32[192]{0:T(256)} %get-tuple-element.75) | copy-start | bytes 2308 | tf_op jit(solution)/shard_map/cond
  105.8 21.1 %copy-start.1 = (bf16[1024,384]{1,0:T(8,128)(2,1)S(1)}, bf16[1024,384]{1,0:T(8,128)(2,1)}, u32[]{:S(2)}) copy-start(bf16[1024,384]{1,0:T(8,128)(2,1)} %copy-done) | copy-start | bytes 2359300 | tf_op jit(solution)/shard_map/cond
  122.4 28.7 %collective-permute-start.16 = (bf16[512,384]{1,0:T(8,128)(2,1)S(1)}, bf16[512,384]{1,0:T(8,128)(2,1)S(1)}, u32[]{:S(2)}, u32[]{:S(2)}) collective-permute-start(bf16[512,384]{1,0:T(8,128)(2,1)S(1)} %slice.48), channel_id=1, source_target_pairs={{0,32},{32,64},{64,96},{96,128},{128,160},{160,192},{192,224},{224... | collective-permute-start | bytes 1179656 | tf_op jit(solution)/shard_map/cond/branch_1_fun/ppermute | solution.py:21
  123.6 27.6 %collective-permute-start.17 = (bf16[512,384]{1,0:T(8,128)(2,1)S(1)}, bf16[512,384]{1,0:T(8,128)(2,1)S(1)}, u32[]{:S(2)}, u32[]{:S(2)}) collective-permute-start(bf16[512,384]{1,0:T(8,128)(2,1)S(1)} %slice.49), channel_id=1, source_target_pairs={{0,224},{32,0},{64,32},{96,64},{128,96},{160,128},{192,160},{224,1... | collective-permute-start | bytes 1179656 | tf_op jit(solution)/shard_map/cond/branch_1_fun/ppermute | solution.py:21
where the time goes:
time: 196 us
  waiting for transfers between devices  98.9 us (50%)
  blocking collectives  33 us (17%)
  Pallas kernels  29.6 us (15%)
  starting transfers between devices  20.3 us (10%)
  local copies, waits for them, and re-layouts  8.71 us (4%)
    ppermute x12, waiting for transfers between devices, shifted(): lax.ppermute(value, axis, [(i, (i + by) % devices) for i in range(devices)])  98.9 us
    pallas_call x3, Pallas kernels, list_terms(): pl.pallas_call(functools.partial(list_kernel, places), grid_spec=pltpu.Pr...  24.5 us
    ppermute x12, starting transfers between devices, shifted(): lax.ppermute(value, axis, [(i, (i + by) % devices) for i in range(devices)])  20.3 us
    all_to_all x1, blocking collectives, spread(): mine = lax.all_to_all(sent, ('ka', 'band'), 0, 0, tiled=True).sum(0)  20 us
    all_gather x1, blocking collectives, spread(): return lax.all_gather(mine, 'fit').sum(0)  13.1 us
    pallas_call x3, Pallas kernels, cut(): pl.pallas_call(functools.partial(cut_kernel, groups), grid_spec=pltpu.Pre...  5.08 us
  transfers between devices with their start and end apart: 12, of which 5 were waited for; matrix products, arithmetic and copies ran while one was open for 3% of the time, Pallas kernels for 11%

commit v1 on v0

--- a/solution.py
+++ b/solution.py
@@ -112,14 +112,16 @@
                         sems.at[which % 2, operand],
                     ).start()
 
-    slot = step % 2
-    for operand in range(2):
-        here = buffer.at[slot, operand]
-        pltpu.make_async_copy(here, here, sems.at[slot, operand]).wait()
-    begins = pairs[BEGINS, step] != 0
-    add_product(buffer.at[slot, 0], buffer.at[slot, 1], w_ref, scaled, total, begins)
-
-    @pl.when(pairs[ENDS, step] != 0)
+    @pl.when(pairs[A, step] >= 0)
+    def _():
+        slot = step % 2
+        for operand in range(2):
+            here = buffer.at[slot, operand]
+            pltpu.make_async_copy(here, here, sems.at[slot, operand]).wait()
+        begins = pairs[BEGINS, step] != 0
+        add_product(buffer.at[slot, 0], buffer.at[slot, 1], w_ref, scaled, total, begins)
+
+    @pl.when((pairs[A, step] >= 0) & (pairs[ENDS, step] != 0))
     def _():
         terms = folded_total(total, fold_ref).reshape(out_ref.shape)
         out_ref[...] = so_far_ref[...] + terms
@@ -261,12 +263,16 @@
 
 def listed_pairs(cycle, distance):
     far = cycle // 2
-
-    def waits(d):
+    groups = [[], [], []]
+    for d in range(cycle):
         blocks = (d, (d + distance) % cycle)
-        return 2 if far in blocks else int(2 in blocks or cycle - 2 in blocks)
-
-    return sorted(range(cycle), key=lambda d: (waits(d), d))
+        late = 2 if far in blocks else int(2 in blocks or cycle - 2 in blocks)
+        groups[late].append((*blocks, d))
+    steps = []
+    for group, length in zip(groups, (4, 4, 2)):
+        idle = (-1, -1, group[-1][2])
+        steps += group + [idle] * (length - len(group))
+    return np.array(steps, np.int32).T
 
 
 def spread(distance, x, coefficients, omega):
@@ -299,25 +305,25 @@
     up_short, up_two, up_long, up_far = ring(up_long, up_short, 1)
     down_short, down_two, down_long, down_far = ring(down_long, down_short, -1)
 
-    firsts = np.array([listed_pairs(cycle, max(t, 1)) for t in range(cycle)], np.int32)
-    firsts = jnp.asarray(firsts)[distance]
-
-    def table(first):
+    listed = np.stack([listed_pairs(cycle, min(max(t, 2), cycle - 2)) for t in range(cycle)])
+    listed = jnp.asarray(listed)[distance]
+
+    def table(begin, end):
+        first, second, place = listed[:, begin:end]
         one, none = jnp.ones_like(first), jnp.zeros_like(first)
-        second, owner = (first + distance) % cycle, (first + me) % cycle
-        return jnp.stack([first, second, owner, one, one, none, none])
+        return jnp.stack([first, second, (place + me) % cycle, one, one, none, none])
 
     views = [[(own, 0)]] * cycle
     views[1], views[7] = [(down_short, size)], [(up_short, size)]
     views[3], views[5] = [(down_long, 0)], [(up_long, 0)]
     terms = jnp.zeros((cycle, owners, rows, NOCC), jnp.float32)
-    terms = list_terms(table(firsts[:2]), views, weights, fold, terms)
+    terms = list_terms(table(0, 4), views, weights, fold, terms)
     up_two, down_two, terms = lax.optimization_barrier((up_two, down_two, terms))
     views[2], views[6] = [(down_two, 0)], [(up_two, 0)]
-    terms = list_terms(table(firsts[2:6]), views, weights, fold, terms)
+    terms = list_terms(table(4, 8), views, weights, fold, terms)
     up_far, down_far, terms = lax.optimization_barrier((up_far, down_far, terms))
     views[4] = [(up_far, 0), (down_far, 0)]
-    terms = list_terms(table(firsts[6:]), views, weights, fold, terms)
+    terms = list_terms(table(8, 10), views, weights, fold, terms)
     sent = terms.reshape(cycle * owners, rows, NOCC)
     mine = lax.all_to_all(sent, ("ka", "band"), 0, 0, tiled=True).sum(0)
     return lax.all_gather(mine, "fit").sum(0)

time: 196 us -> 192 us (0.980); the launches traced: 196 us -> 194 us
  local copies, waits for them, and re-layouts: 8.71 us -> 5.25 us
  waiting for transfers between devices: 98.9 us -> 102 us
  blocking collectives: 33 us -> 31 us
    ppermute x12, waiting for transfers between devices: 98.9 us -> 102 us  [shifted(): lax.ppermute(value, axis, [(i, (i + by) % devices) for i in range(devices)])]
  transfers between devices with their start and end apart: 12 -> 12, of which waited for: 5 -> 5; matrix products, arithmetic and copies ran while one was open for 3% -> 2% of each run, Pallas kernels for 11% -> 11%
where the time goes in v1:
time: 192 us; the launch traced here: 194 us
  waiting for transfers between devices  102 us (53%)
  blocking collectives  31 us (16%)
  Pallas kernels  28.9 us (15%)
  starting transfers between devices  22 us (11%)
  local copies, waits for them, and re-layouts  5.25 us (3%)
  other arithmetic  2.02 us (1%)
  between operations  1.94 us (1%)
    ppermute x12, waiting for transfers between devices, shifted(): lax.ppermute(value, axis, [(i, (i + by) % devices) for i in range(devices)])  102 us
    pallas_call x3, Pallas kernels, list_terms(): pl.pallas_call(functools.partial(list_kernel, places), grid_spec=pltpu.Pr...  23.8 us
    ppermute x12, starting transfers between devices, shifted(): lax.ppermute(value, axis, [(i, (i + by) % devices) for i in range(devices)])  22 us
    all_to_all x1, blocking collectives, spread(): mine = lax.all_to_all(sent, ('ka', 'band'), 0, 0, tiled=True).sum(0)  18.3 us
    all_gather x1, blocking collectives, spread(): return lax.all_gather(mine, 'fit').sum(0)  12.7 us
    pallas_call x3, Pallas kernels, cut(): pl.pallas_call(functools.partial(cut_kernel, groups), grid_spec=pltpu.Pre...  5.07 us
  transfers between devices with their start and end apart: 12, of which 5 were waited for; matrix products, arithmetic and copies ran while one was open for 2% of the time, Pallas kernels for 11%

profile of v1, /device:TPU:1, one launch (start us, length us, event | category | flops | bytes accessed | tf_op | source)
XLA Modules:
  0.0 194.5 jit_solution(15054025011063230296)
XLA Ops:
  1.9 191.3 %conditional.1 = (f32[24,48]{1,0:T(8,128)S(1)}) conditional(s32[]{:T(128)} %convert_element_type.9, (s32[]{:T(128)}, (), (), (), (), /*index=5*/bf16[1024,3072]{1,0:T(8,128)(2,1)}, f32[6,512]{1,0:T(8,128)}, f32[2,6]{1,0:T(2,128)}, s32[1536]{0:T(1024)}, s32[192]{0:T(256)}, /*index=10*/(), (), (), ()) %tuple.69, (s32[]{:T(128)}, (), ...), branch_computations={%region_0.2_spmd, %region_2.5_spmd} | conditional | flops 740944 | bytes 83907912 | solution.py:337
  2.0 1.8 cut.9
  3.8 6.5 %collective-permute-start.10 = (bf16[1536,384]{1,0:T(8,128)(2,1)S(1)}, bf16[1536,384]{1,0:T(8,128)(2,1)}, u32[]{:S(2)}, u32[]{:S(2)}) collective-permute-start(bf16[1536,384]{1,0:T(8,128)(2,1)S(1)} %get-tuple-element.68), channel_id=1, source_target_pairs={{0,224},{32,0},{64,32},{96,64},{128,96},{160,128},{192,160},{224,1... | collective-permute-start | bytes 3538952 | tf_op jit(solution)/shard_map/cond/branch_1_fun/ppermute | solution.py:21
  10.3 2.1 %cut.8 = (bf16[2048,384]{1,0:T(8,128)(2,1)}, bf16[2048,384]{1,0:T(8,128)(2,1)}) custom-call(s32[1]{0:T(128)} %bitcast.5.me_ref, bf16[1024,3072]{1,0:T(8,128)(2,1)S(1)} %copy-done.1), custom_call_target="tpu_custom_call" | custom-call | tf_op jit(solution)/shard_map/cond/branch_1_fun/cut/pallas_call | solution.py:192
  12.4 22.5 %collective-permute-done.10 = bf16[1536,384]{1,0:T(8,128)(2,1)} collective-permute-done((bf16[1536,384]{1,0:T(8,128)(2,1)S(1)}, bf16[1536,384]{1,0:T(8,128)(2,1)}, u32[]{:S(2)}, u32[]{:S(2)}) %collective-permute-start.10) | collective-permute-done | bytes 1179680 | tf_op jit(solution)/shard_map/cond/branch_1_fun/ppermute | solution.py:21
  34.9 3.5 %collective-permute-start.11 = (bf16[1536,384]{1,0:T(8,128)(2,1)}, bf16[1536,384]{1,0:T(8,128)(2,1)}, u32[]{:S(2)}, u32[]{:S(2)}) collective-permute-start(bf16[1536,384]{1,0:T(8,128)(2,1)} %collective-permute-done.10), channel_id=1, source_target_pairs={{0,224},{32,0},{64,32},{96,64},{128,96},{160,128},{192,160},{224,1... | collective-permute-start | bytes 3538952 | tf_op jit(solution)/shard_map/cond/branch_1_fun/ppermute | solution.py:21
  38.4 2.7 %collective-permute-start.6 = (bf16[2048,384]{1,0:T(8,128)(2,1)}, bf16[2048,384]{1,0:T(8,128)(2,1)}, u32[]{:S(2)}, u32[]{:S(2)}) collective-permute-start(bf16[2048,384]{1,0:T(8,128)(2,1)} %get-tuple-element.66), channel_id=1, source_target_pairs={{0,224},{32,0},{64,32},{96,64},{128,96},{160,128},{192,160},{224,1... | collective-permute-start | bytes 4718600 | tf_op jit(solution)/shard_map/cond/branch_1_fun/ppermute | solution.py:21
  41.2 0.7 dynamic-slice_bitcast_fusion
  41.9 20.5 %collective-permute-done.11 = bf16[1536,384]{1,0:T(8,128)(2,1)} collective-permute-done((bf16[1536,384]{1,0:T(8,128)(2,1)}, bf16[1536,384]{1,0:T(8,128)(2,1)}, u32[]{:S(2)}, u32[]{:S(2)}) %collective-permute-start.11) | collective-permute-done | bytes 1179680 | tf_op jit(solution)/shard_map/cond/branch_1_fun/ppermute | solution.py:21
  62.4 3.4 %collective-permute-start.12 = (bf16[1536,384]{1,0:T(8,128)(2,1)}, bf16[1536,384]{1,0:T(8,128)(2,1)S(1)}, u32[]{:S(2)}, u32[]{:S(2)}) collective-permute-start(bf16[1536,384]{1,0:T(8,128)(2,1)} %collective-permute-done.11), channel_id=1, source_target_pairs={{0,224},{32,0},{64,32},{96,64},{128,96},{160,128},{192,160},{224,1... | collective-permute-start | bytes 3538952 | tf_op jit(solution)/shard_map/cond/branch_1_fun/ppermute | solution.py:21
  66.4 32.8 %collective-permute-done.7.refs_4_.refs_6_.refs_8_ = bf16[2048,384]{1,0:T(8,128)(2,1)S(1)} collective-permute-done((bf16[2048,384]{1,0:T(8,128)(2,1)}, bf16[2048,384]{1,0:T(8,128)(2,1)S(1)}, u32[]{:S(2)}, u32[]{:S(2)}) %collective-permute-start.7) | collective-permute-done | bytes 1572896 | tf_op jit(solution)/shard_map/cond/branch_1_fun/ppermute | solution.py:21
  99.3 0.1 collective-permute-start.8
  99.4 1.2 slice.50
  100.6 2.7 %collective-permute-start.9 = (bf16[1024,384]{1,0:T(8,128)(2,1)S(1)}, bf16[1024,384]{1,0:T(8,128)(2,1)S(1)}, u32[]{:S(2)}, u32[]{:S(2)}) collective-permute-start(bf16[1024,384]{1,0:T(8,128)(2,1)S(1)} %slice.50), channel_id=1, source_target_pairs={{0,224},{32,0},{64,32},{96,64},{128,96},{160,128},{192,160},{224,1... | collective-permute-start | bytes 2359304 | tf_op jit(solution)/shard_map/cond/branch_1_fun/ppermute | solution.py:21
  103.4 1.2 cut.7.refs_0_
  104.6 0.6 convolution_multiply_fusion.1.refs_5_.refs_7_.refs_9_
  105.2 19.2 %collective-permute-done.15.refs_3_.refs_4_.refs_6_ = bf16[1536,384]{1,0:T(8,128)(2,1)S(1)} collective-permute-done((bf16[1536,384]{1,0:T(8,128)(2,1)}, bf16[1536,384]{1,0:T(8,128)(2,1)S(1)}, u32[]{:S(2)}, u32[]{:S(2)}) %collective-permute-start.15) | collective-permute-done | bytes 1179680 | tf_op jit(solution)/shard_map/cond/branch_1_fun/ppermute | solution.py:21
  124.6 3.0 %collective-permute-start.17 = (bf16[512,384]{1,0:T(8,128)(2,1)S(1)}, bf16[512,384]{1,0:T(8,128)(2,1)S(1)}, u32[]{:S(2)}, u32[]{:S(2)}) collective-permute-start(bf16[512,384]{1,0:T(8,128)(2,1)S(1)} %slice.52), channel_id=1, source_target_pairs={{0,224},{32,0},{64,32},{96,64},{128,96},{160,128},{192,160},{224,1... | collective-permute-start | bytes 1179656 | tf_op jit(solution)/shard_map/cond/branch_1_fun/ppermute | solution.py:21
  127.6 0.3 compare_convert_fusion.1.refs_6_.refs_8_.refs_10_
  128.0 6.2 %list_terms.7.refs_9_ = f32[8,8,24,48]{3,2,1,0:T(8,128)S(1)} custom-call(s32[7,4]{1,0:T(8,128)S(1)} %get-tuple-element.113.pairs, bf16[1024,384]{1,0:T(8,128)(2,1)S(1)} %cut.7.refs_0_, bf16[2048,384]{1,0:T(8,128)(2,1)} %collective-permute-done.6.refs_1_, ...), custom_call_target="tpu_custom_call", output_to_operand_aliasing={{}: (8, {})} | custom-call | tf_op jit(solution)/shard_map/cond/branch_1_fun/list_terms/pallas_call | solution.py:144
  134.2 7.1 %collective-permute-done.8.refs_5_.refs_7_ = bf16[1024,384]{1,0:T(8,128)(2,1)S(1)} collective-permute-done((bf16[1024,384]{1,0:T(8,128)(2,1)S(1)}, bf16[1024,384]{1,0:T(8,128)(2,1)S(1)}, u32[]{:S(2)}, u32[]{:S(2)}) %collective-permute-start.8) | collective-permute-done | bytes 786464 | tf_op jit(solution)/shard_map/cond/branch_1_fun/ppermute | solution.py:21
  141.3 11.0 %list_terms.8.refs_11_ = f32[8,8,24,48]{3,2,1,0:T(8,128)S(1)} custom-call(s32[7,4]{1,0:T(8,128)S(1)} %get-tuple-element.112.pairs, bf16[1024,384]{1,0:T(8,128)(2,1)S(1)} %cut.7.refs_0_, bf16[2048,384]{1,0:T(8,128)(2,1)} %collective-permute-done.6.refs_1_, bf16[1024,384]{1,0:T(8,128)(2,1)S(1)} %collective-permute-done.9.refs_2_, ...), custom_call_target="tpu_custom_call", output_to_operand_aliasing={{}: (10, {})} | custom-call | tf_op jit(solution)/shard_map/cond/branch_1_fun/list_terms/pallas_call | solution.py:144
  152.4 6.6 %list_terms.9 = f32[8,8,24,48]{3,2,1,0:T(8,128)S(1)} custom-call(s32[7,2]{1,0:T(8,128)S(1)} %add_add_fusion.pairs, bf16[1024,384]{1,0:T(8,128)(2,1)S(1)} %cut.7.refs_0_, bf16[2048,384]{1,0:T(8,128)(2,1)} %collective-permute-done.6.refs_1_, bf16[1024,384]{1,0:T(8,128)(2,1)S(1)} %collective-permute-done.9.refs_2_, ...), custom_call_target="tpu_custom_call", output_to_operand_aliasing={{}: (12, {})} | custom-call | tf_op jit(solution)/shard_map/cond/branch_1_fun/list_terms/pallas_call | solution.py:144
  159.0 0.7 reshape.38
  159.7 18.3 %all_to_all.9 = f32[64,1,1152]{2,1,0:T(1,128)S(1)} all-to-all(f32[64,1,1152]{2,1,0:T(1,128)S(1)} %reshape.38), channel_id=1, replica_groups=mesh['ka'=8,'band'=8,'fit'=4] {'ka','band'}, dimensions={0} | all-to-all | bytes 589824 | tf_op jit(solution)/shard_map/cond/branch_1_fun/all_to_all | solution.py:328
  178.0 0.5 broadcast.81
  178.6 1.3 reduce.1
  179.9 0.3 reshape.39
  180.2 0.1 reduce_sum.25
  180.3 12.7 %all-gather = f32[96,48]{1,0:T(8,128)S(1)} all-gather(f32[24,48]{1,0:T(8,128)S(1)} %reduce_sum.25), channel_id=2, replica_groups=mesh['ka'=8,'band'=8,'fit'=4] {'fit'}, dimensions={0}, use_global_device_ids=true | all-gather | bytes 23040 | tf_op jit(solution)/shard_map/cond/branch_1_fun/all_gather | solution.py:329
  193.3 0.6 squeeze.17
  193.9 0.6 squeeze.18
  (40 shorter events, 1.0 us)
Async XLA Ops:
  1.9 8.3 %copy-start.1 = (bf16[1024,3072]{1,0:T(8,128)(2,1)S(1)}, bf16[1024,3072]{1,0:T(8,128)(2,1)}, u32[]{:S(2)}) copy-start(bf16[1024,3072]{1,0:T(8,128)(2,1)} %get-tuple-element.65.x_ref) | copy-start | bytes 18874372 | tf_op jit(solution)/shard_map/cond
  3.8 31.1 %collective-permute-start.10 = (bf16[1536,384]{1,0:T(8,128)(2,1)S(1)}, bf16[1536,384]{1,0:T(8,128)(2,1)}, u32[]{:S(2)}, u32[]{:S(2)}) collective-permute-start(bf16[1536,384]{1,0:T(8,128)(2,1)S(1)} %get-tuple-element.68), channel_id=1, source_target_pairs={{0,224},{32,0},{64,32},{96,64},{128,96},{160,128},{192,160},{224,1... | collective-permute-start | bytes 3538952 | tf_op jit(solution)/shard_map/cond/branch_1_fun/ppermute | solution.py:21
  10.3 30.9 %copy-start.19 = (s32[]{:T(128)S(1)}, s32[]{:T(128)}, u32[]{:S(2)}) copy-start(s32[]{:T(128)} %get-tuple-element.64) | copy-start | bytes 16 | tf_op jit(solution)/shard_map/cond
  10.3 28.2 %collective-permute-start.13 = (bf16[1536,384]{1,0:T(8,128)(2,1)S(1)}, bf16[1536,384]{1,0:T(8,128)(2,1)}, u32[]{:S(2)}, u32[]{:S(2)}) collective-permute-start(bf16[1536,384]{1,0:T(8,128)(2,1)S(1)} %get-tuple-element.70), channel_id=1, source_target_pairs={{0,32},{32,64},{64,96},{96,128},{128,160},{160,192},{192,224},{224... | collective-permute-start | bytes 3538952 | tf_op jit(solution)/shard_map/cond/branch_1_fun/ppermute | solution.py:21
  34.9 27.5 %collective-permute-start.11 = (bf16[1536,384]{1,0:T(8,128)(2,1)}, bf16[1536,384]{1,0:T(8,128)(2,1)}, u32[]{:S(2)}, u32[]{:S(2)}) collective-permute-start(bf16[1536,384]{1,0:T(8,128)(2,1)} %collective-permute-done.10), channel_id=1, source_target_pairs={{0,224},{32,0},{64,32},{96,64},{128,96},{160,128},{192,160},{224,1... | collective-permute-start | bytes 3538952 | tf_op jit(solution)/shard_map/cond/branch_1_fun/ppermute | solution.py:21
  38.4 27.4 %collective-permute-start.14 = (bf16[1536,384]{1,0:T(8,128)(2,1)}, bf16[1536,384]{1,0:T(8,128)(2,1)}, u32[]{:S(2)}, u32[]{:S(2)}) collective-permute-start(bf16[1536,384]{1,0:T(8,128)(2,1)} %collective-permute-done.13), channel_id=1, source_target_pairs={{0,32},{32,64},{64,96},{96,128},{128,160},{160,192},{192,224},{224... | collective-permute-start | bytes 3538952 | tf_op jit(solution)/shard_map/cond/branch_1_fun/ppermute | solution.py:21
  38.4 60.8 %collective-permute-start.7 = (bf16[2048,384]{1,0:T(8,128)(2,1)}, bf16[2048,384]{1,0:T(8,128)(2,1)S(1)}, u32[]{:S(2)}, u32[]{:S(2)}) collective-permute-start(bf16[2048,384]{1,0:T(8,128)(2,1)} %get-tuple-element.67), channel_id=1, source_target_pairs={{0,32},{32,64},{64,96},{96,128},{128,160},{160,192},{192,224},{224... | collective-permute-start | bytes 4718600 | tf_op jit(solution)/shard_map/cond/branch_1_fun/ppermute | solution.py:21
  38.4 60.9 %collective-permute-start.6 = (bf16[2048,384]{1,0:T(8,128)(2,1)}, bf16[2048,384]{1,0:T(8,128)(2,1)}, u32[]{:S(2)}, u32[]{:S(2)}) collective-permute-start(bf16[2048,384]{1,0:T(8,128)(2,1)} %get-tuple-element.66), channel_id=1, source_target_pairs={{0,224},{32,0},{64,32},{96,64},{128,96},{160,128},{192,160},{224,1... | collective-permute-start | bytes 4718600 | tf_op jit(solution)/shard_map/cond/branch_1_fun/ppermute | solution.py:21
  62.4 62.2 %collective-permute-start.12 = (bf16[1536,384]{1,0:T(8,128)(2,1)}, bf16[1536,384]{1,0:T(8,128)(2,1)S(1)}, u32[]{:S(2)}, u32[]{:S(2)}) collective-permute-start(bf16[1536,384]{1,0:T(8,128)(2,1)} %collective-permute-done.11), channel_id=1, source_target_pairs={{0,224},{32,0},{64,32},{96,64},{128,96},{160,128},{192,160},{224,1... | collective-permute-start | bytes 3538952 | tf_op jit(solution)/shard_map/cond/branch_1_fun/ppermute | solution.py:21
  65.8 58.6 %collective-permute-start.15 = (bf16[1536,384]{1,0:T(8,128)(2,1)}, bf16[1536,384]{1,0:T(8,128)(2,1)S(1)}, u32[]{:S(2)}, u32[]{:S(2)}) collective-permute-start(bf16[1536,384]{1,0:T(8,128)(2,1)} %collective-permute-done.14), channel_id=1, source_target_pairs={{0,32},{32,64},{64,96},{96,128},{128,160},{160,192},{192,224},{224... | collective-permute-start | bytes 3538952 | tf_op jit(solution)/shard_map/cond/branch_1_fun/ppermute | solution.py:21
  99.3 42.0 %collective-permute-start.8 = (bf16[1024,384]{1,0:T(8,128)(2,1)S(1)}, bf16[1024,384]{1,0:T(8,128)(2,1)S(1)}, u32[]{:S(2)}, u32[]{:S(2)}) collective-permute-start(bf16[1024,384]{1,0:T(8,128)(2,1)S(1)} %slice.49), channel_id=1, source_target_pairs={{0,32},{32,64},{64,96},{96,128},{128,160},{160,192},{192,224},{224... | collective-permute-start | bytes 2359304 | tf_op jit(solution)/shard_map/cond/branch_1_fun/ppermute | solution.py:21
  100.6 40.7 %collective-permute-start.9 = (bf16[1024,384]{1,0:T(8,128)(2,1)S(1)}, bf16[1024,384]{1,0:T(8,128)(2,1)S(1)}, u32[]{:S(2)}, u32[]{:S(2)}) collective-permute-start(bf16[1024,384]{1,0:T(8,128)(2,1)S(1)} %slice.50), channel_id=1, source_target_pairs={{0,224},{32,0},{64,32},{96,64},{128,96},{160,128},{192,160},{224,1... | collective-permute-start | bytes 2359304 | tf_op jit(solution)/shard_map/cond/branch_1_fun/ppermute | solution.py:21
  103.4 1.2 copy-start.3
  103.4 1.2 copy-start.7
  104.6 23.1 %copy-start.5 = (s32[1536]{0:T(1024)S(1)}, s32[1536]{0:T(1024)}, u32[]{:S(2)}) copy-start(s32[1536]{0:T(1024)} %get-tuple-element.74) | copy-start | bytes 18436 | tf_op jit(solution)/shard_map/cond
  104.6 23.0 %copy-start.9 = (s32[192]{0:T(256)S(1)}, s32[192]{0:T(256)}, u32[]{:S(2)}) copy-start(s32[192]{0:T(256)} %get-tuple-element.75) | copy-start | bytes 2308 | tf_op jit(solution)/shard_map/cond
  124.5 27.9 %collective-permute-start.16 = (bf16[512,384]{1,0:T(8,128)(2,1)S(1)}, bf16[512,384]{1,0:T(8,128)(2,1)S(1)}, u32[]{:S(2)}, u32[]{:S(2)}) collective-permute-start(bf16[512,384]{1,0:T(8,128)(2,1)S(1)} %slice.51), channel_id=1, source_target_pairs={{0,32},{32,64},{64,96},{96,128},{128,160},{160,192},{192,224},{224... | collective-permute-start | bytes 1179656 | tf_op jit(solution)/shard_map/cond/branch_1_fun/ppermute | solution.py:21
  124.6 27.7 %collective-permute-start.17 = (bf16[512,384]{1,0:T(8,128)(2,1)S(1)}, bf16[512,384]{1,0:T(8,128)(2,1)S(1)}, u32[]{:S(2)}, u32[]{:S(2)}) collective-permute-start(bf16[512,384]{1,0:T(8,128)(2,1)S(1)} %slice.52), channel_id=1, source_target_pairs={{0,224},{32,0},{64,32},{96,64},{128,96},{160,128},{192,160},{224,1... | collective-permute-start | bytes 1179656 | tf_op jit(solution)/shard_map/cond/branch_1_fun/ppermute | solution.py:21
